TPU v7x, 32 devices: a whole 2x2x4 slice. The times are simulated.
32 devices in a mesh: user: 16 (over z, x, core), tensor: 2 (over y).
Axes of the slice: x: 2, y: 2, z: 4, core: 2. Of those that a mesh axis runs over, the one named last changes fastest.
Arguments:
- events: bfloat16 [256, 128, 1024], P('user', None, 'tensor'), may hold values from -6 to 6
- cotangent: bfloat16 [256, 128, 1024], P('user', None, 'tensor'), may hold values from -6 to 6
- w_in: bfloat16 [1024, 4096], P('user', 'tensor'), may hold values from -0.1875 to 0.1875
- w_out: bfloat16 [1024, 1024], P('user', 'tensor'), may hold values from -0.1875 to 0.1875
- slot_source: int32 [256], P('user'), may hold values from 0 to 15, as said below
- slot_length: int32 [256], P('user'), may hold values from 1 to 127, as said below
Outputs:
- grad_x: bfloat16 [256, 128, 1024], P('user', None, 'tensor')
- grad_w_in: float32 [1024, 4096], P('user', 'tensor')
- grad_w_out: float32 [1024, 1024], P('user', 'tensor')
Inputs may be any that keep to these rules, and one draw needn't show every extreme that they name: `slot_source`: the 16 slots of one host name distinct user shards, and for each slot j the entries h * 16 + j over all hosts h name every user shard once, so every history is placed exactly once. `slot_length`: the 16 slot lengths of one host sum to 1024.
All inputs are finite; a program needn't handle non-finite values.
Results may differ from a plain program's by a relative error of at most 0.023.
Values may be sent and summed in bfloat16 or wider, within the bound.
No kernel may reach another device: no remote copies, remote signals or barrier semaphores. Data moves between devices by JAX's collectives and lax.ppermute only.
A program may use at most 128 MiB of HBM per device.

v0:
```python
import math

import jax
import jax.numpy as jnp
from jax import lax
from jax.sharding import PartitionSpec as P

D = 1024
HEAD_DIM = 128
SEQ_LEN = 128


eps = 1e-05


def silu_grad(t):
    sig = jax.nn.sigmoid(t)
    return sig * (1.0 + t * (1.0 - sig))


def host_rows(lengths, sources, total_rows, hist):
    ends = jnp.cumsum(lengths)
    starts = ends - lengths
    rows = jnp.arange(total_rows, dtype=jnp.int32)
    segment = jnp.sum((rows[:, None] >= ends[None, :]).astype(jnp.int32), axis=1)
    onehot = (segment[:, None] == jnp.arange(hist, dtype=jnp.int32)[None, :]).astype(jnp.int32)
    position = rows - jnp.sum(onehot * starts[None, :], axis=1)
    source = jnp.sum(onehot * sources[None, :], axis=1)
    return (segment, position, source, starts)


def local(events, cotangent, w_in, w_out, slot_source, slot_length):
    users = lax.axis_size("user")
    hist, seq_len, width_part = events.shape
    total_rows = hist // 2 * seq_len
    table = lax.all_gather(slot_source, "user", axis=0, tiled=True).reshape(users, hist)
    myself = lax.axis_index("user")
    matches = (table == myself).astype(jnp.int32)
    host_ids = jnp.arange(users, dtype=jnp.int32)[:, None]
    host_of = jnp.sum(matches * host_ids, axis=0)
    send_x = jnp.zeros_like(events).at[host_of].set(events)
    send_d = jnp.zeros_like(cotangent).at[host_of].set(cotangent)
    recv_x, recv_d = (
        lax.all_to_all(send_x, "user", split_axis=0, concat_axis=0, tiled=True),
        lax.all_to_all(send_d, "user", split_axis=0, concat_axis=0, tiled=True),
    )
    segment, position, source, starts = host_rows(slot_length, slot_source, total_rows, hist)
    index = source * seq_len + position
    xp = jnp.take(recv_x.reshape(users * seq_len, width_part), index, axis=0)
    dp = jnp.take(recv_d.reshape(users * seq_len, width_part), index, axis=0)
    x_full, d_full = (
        lax.all_gather(xp, "tensor", axis=1, tiled=True),
        lax.all_gather(dp, "tensor", axis=1, tiled=True),
    )
    w_in_cols = lax.all_gather(w_in, "user", axis=0, tiled=True)
    w_out_cols = lax.all_gather(w_out, "user", axis=0, tiled=True)
    xf = x_full.astype(jnp.float32)
    centred = xf - jnp.mean(xf, axis=1, keepdims=True)
    rstd = lax.rsqrt(jnp.mean(centred * centred, axis=1, keepdims=True) + eps)
    nf = centred * rstd
    nb = nf.astype(jnp.bfloat16)
    z = jnp.dot(nb, w_in_cols, preferred_element_type=jnp.float32)
    local_heads = w_in_cols.shape[1] // (4 * HEAD_DIM)
    g = (
        jax.nn.silu(z)
        .astype(jnp.bfloat16)
        .reshape(total_rows, local_heads, 4, HEAD_DIM)
        .transpose(1, 2, 0, 3)
    )
    upart, vpart, qpart, kpart = (g[:, 0], g[:, 1], g[:, 2], g[:, 3])
    dh = (
        jnp.dot(d_full, w_out_cols, preferred_element_type=jnp.float32)
        .reshape(total_rows, local_heads, HEAD_DIM)
        .transpose(1, 0, 2)
    )
    scale = HEAD_DIM ** (-0.5)
    block = math.gcd(total_rows, 512)
    hparts, grads_u, grads_q = ([], [], [])
    grad_v = jnp.zeros((local_heads, total_rows, HEAD_DIM), jnp.float32)
    grad_k = jnp.zeros((local_heads, total_rows, HEAD_DIM), jnp.float32)
    for number in range(total_rows // block):
        lo = number * block
        hi = lo + block
        mask = (segment[lo:hi, None] == segment[None, :]) & (
            position[None, :] <= position[lo:hi, None]
        )
        q_rows = qpart[:, lo:hi]
        scores = (
            jnp.einsum("hqe,hke->hqk", q_rows, kpart, preferred_element_type=jnp.float32) * scale
        )
        attn = jnp.where(mask[None], jax.nn.silu(scores) / SEQ_LEN, 0.0).astype(jnp.bfloat16)
        yval = jnp.einsum("hqk,hke->hqe", attn, vpart, preferred_element_type=jnp.float32)
        ycen = yval - jnp.mean(yval, axis=2, keepdims=True)
        yrstd = lax.rsqrt(jnp.mean(ycen * ycen, axis=2, keepdims=True) + eps)
        ynorm = ycen * yrstd
        uf = upart[:, lo:hi].astype(jnp.float32)
        hparts.append((ynorm * uf).astype(jnp.bfloat16))
        grad_h = dh[:, lo:hi]
        grads_u.append(grad_h * ynorm)
        grad_yn = grad_h * uf
        grad_y = (
            (
                grad_yn
                - jnp.mean(grad_yn, axis=2, keepdims=True)
                - ynorm * jnp.mean(grad_yn * ynorm, axis=2, keepdims=True)
            )
            * yrstd
        ).astype(jnp.bfloat16)
        grad_a = jnp.einsum("hqe,hke->hqk", grad_y, vpart, preferred_element_type=jnp.float32)
        grad_v = grad_v + jnp.einsum(
            "hqk,hqe->hke", attn, grad_y, preferred_element_type=jnp.float32
        )
        grad_s = jnp.where(mask[None], grad_a * silu_grad(scores) * (scale / SEQ_LEN), 0.0).astype(
            jnp.bfloat16
        )
        grads_q.append(
            jnp.einsum("hqk,hke->hqe", grad_s, kpart, preferred_element_type=jnp.float32)
        )
        grad_k = grad_k + jnp.einsum(
            "hqk,hqe->hke", grad_s, q_rows, preferred_element_type=jnp.float32
        )
    hb = (
        jnp.concatenate(hparts, axis=1)
        .transpose(1, 0, 2)
        .reshape(total_rows, local_heads * HEAD_DIM)
    )
    grad_u = jnp.concatenate(grads_u, axis=1)
    grad_q = jnp.concatenate(grads_q, axis=1)
    dgrad = (
        jnp.stack([grad_u, grad_v, grad_q, grad_k], axis=1)
        .transpose(2, 0, 1, 3)
        .reshape(total_rows, 4 * local_heads * HEAD_DIM)
    )
    dz = (dgrad * silu_grad(z)).astype(jnp.bfloat16)
    columns = d_full
    grad_w_out = lax.psum_scatter(
        lax.dot_general(
            columns, hb, (((0,), (0,)), ((), ())), preferred_element_type=jnp.float32
        ).astype(jnp.bfloat16),
        "user",
        scatter_dimension=0,
        tiled=True,
    ).astype(jnp.float32)
    columns = nb
    grad_w_in = lax.psum_scatter(
        lax.dot_general(
            columns, dz, (((0,), (0,)), ((), ())), preferred_element_type=jnp.float32
        ).astype(jnp.bfloat16),
        "user",
        scatter_dimension=0,
        tiled=True,
    ).astype(jnp.float32)
    dn = lax.dot_general(
        dz, w_in_cols, (((1,), (1,)), ((), ())), preferred_element_type=jnp.float32
    )
    first_col = lax.axis_index("tensor") * width_part
    n_share = lax.dynamic_slice_in_dim(nf, first_col, width_part, 1)
    dn_share = lax.psum_scatter(dn, "tensor", scatter_dimension=1, tiled=True)
    total_one, total_two = lax.psum(
        (jnp.sum(dn_share, axis=1), jnp.sum(dn_share * n_share, axis=1)), "tensor"
    )
    mean_one = (total_one / D)[:, None]
    mean_two = (total_two / D)[:, None]
    branch = (dn_share - mean_one - n_share * mean_two) * rstd
    dxp = (dp.astype(jnp.float32) + branch).astype(jnp.bfloat16)
    slots = jnp.arange(seq_len, dtype=jnp.int32)
    rows_at = jnp.minimum(starts[:, None] + slots[None, :], total_rows - 1)
    valid = slots[None, :] < slot_length[:, None]
    padded = jnp.take(dxp, rows_at.reshape(-1), axis=0).reshape(hist, seq_len, width_part)
    padded = jnp.where(valid[:, :, None], padded, jnp.zeros_like(padded))
    back = jnp.zeros((users, seq_len, width_part), jnp.bfloat16).at[slot_source].set(padded)
    returned = lax.all_to_all(back, "user", split_axis=0, concat_axis=0, tiled=True)
    grad_x = jnp.take(returned, host_of, axis=0)
    return (grad_x, grad_w_in, grad_w_out)


def solution(mesh):
    in_specs = (
        P("user", None, "tensor"),
        P("user", None, "tensor"),
        P("user", "tensor"),
        P("user", "tensor"),
        P("user"),
        P("user"),
    )
    out_specs = (P("user", None, "tensor"), P("user", "tensor"), P("user", "tensor"))
    return jax.shard_map(local, mesh=mesh, in_specs=in_specs, out_specs=out_specs, check_vma=False)
```

profile of v0, /device:TPU:0, one launch (start us, length us, event | category | flops | bytes accessed | tf_op | source)
XLA Modules:
  0.0 617.8 jit_solution(2139399516039388893)
XLA Ops:
  9.9 13.7 %all-reduce = s32[256]{0:T(256)S(1)} all-reduce(s32[256]{0:T(256)S(1)} %dynamic-update-slice), channel_id=1, replica_groups=mesh['user'=16,'tensor'=2] {'user'}, use_global_device_ids=true, to_apply=%add | all-reduce | flops 256 | bytes 2048
  25.3 5.9 scatter_fusion
  31.2 3.7 all-to-all-start
  36.4 6.0 scatter_fusion.1
  42.4 33.6 %all-to-all-done = bf16[16,128,512]{2,1,0:T(8,128)(2,1)S(1)} async-done(((bf16[16,128,512]{2,1,0:T(8,128)(2,1)}), bf16[16,128,512]{2,1,0:T(8,128)(2,1)S(1)}, u32[]{:S(2)}, u32[]{:S(2)}) %all-to-all-start) | async-done | bytes 2097184 | tf_op jit(solution)/shard_map/all_to_all | solution.py:45
  76.0 11.2 %all-to-all-start.1 = ((bf16[16,128,512]{2,1,0:T(8,128)(2,1)}), bf16[16,128,512]{2,1,0:T(8,128)(2,1)}, u32[]{:S(2)}, u32[]{:S(2)}) async-start(bf16[16,128,512]{2,1,0:T(8,128)(2,1)} %scatter_fusion.1), calls=%async_computation.1 | async-start | bytes 4194304 | tf_op jit(solution)/shard_map/all_to_all | solution.py:44
  88.8 4.0 gather_fusion.2
  92.7 37.7 %all-to-all-done.1 = bf16[16,128,512]{2,1,0:T(8,128)(2,1)} async-done(((bf16[16,128,512]{2,1,0:T(8,128)(2,1)}), bf16[16,128,512]{2,1,0:T(8,128)(2,1)}, u32[]{:S(2)}, u32[]{:S(2)}) %all-to-all-start.1) | async-done | bytes 2097184 | tf_op jit(solution)/shard_map/all_to_all | solution.py:44
  130.5 5.9 gather_fusion.3
  141.3 4.3 all-gather.7.cloned.1.call-done
  145.6 35.2 %all-gather.5.cloned.1.call-done = bf16[1024,1024]{1,0:T(8,128)(2,1)} async-done(((bf16[1024,512]{1,0:T(8,128)(2,1)}), bf16[1024,1024]{1,0:T(8,128)(2,1)}) %all-gather.5.cloned.1.call-update) | async-done | bytes 2097168 | tf_op jit(solution)/shard_map/all_gather | solution.py:53
  180.8 3.2 fusion.29
  185.7 29.7 %all-gather.9.cloned.1.call-done = bf16[1024,1024]{1,0:T(8,128)(2,1)} async-done(((bf16[1024,512]{1,0:T(8,128)(2,1)}), bf16[1024,1024]{1,0:T(8,128)(2,1)}) %all-gather.9.cloned.1.call-update) | async-done | bytes 2097168 | tf_op jit(solution)/shard_map/all_gather | solution.py:52
  215.5 2.1 convert_reduce_fusion
  217.6 2.3 fusion.2
  219.9 48.4 %all-gather.11.cloned.1.call-done = bf16[1024,2048]{1,0:T(8,128)(2,1)} async-done(((bf16[64,2048]{1,0:T(8,128)(2,1)}), bf16[1024,2048]{1,0:T(8,128)(2,1)}) %all-gather.11.cloned.1.call-update) | async-done | bytes 4194320 | tf_op jit(solution)/shard_map/all_gather | solution.py:55
  268.3 10.6 %multiply_convert_fusion.1 = (bf16[1024,2048]{1,0:T(8,128)(2,1)}, f32[1024,2048]{1,0:T(8,128)}) fusion(bf16[1024,2048]{1,0:T(8,128)(2,1)} %all-gather.11.cloned.1.call-done, f32[1024]{0:T(1024)S(1)} %add_rsqrt_fusion.2, f32[1024]{0:T(1024)S(1)} %broadcast_multiply_fusion.8, bf16[1024,1024]{1,0:T(8,128)(2,1)S(1)} %copy-done), kind=kOutput, calls=%fused_computation.15 | convolution fusion | flops 4309647360 | bytes 18882560 | tf_op jit(solution)/shard_map/dot_general | solution.py:62
  278.8 7.7 %reshape.318 = bf16[1024,4,4,128]{3,2,1,0:T(4,128)(2,1)} reshape(bf16[1024,2048]{1,0:T(8,128)(2,1)} %get-tuple-element.34) | data formatting | bytes 8388608 | tf_op jit(solution)/shard_map/reshape | solution.py:67
  286.6 3.3 copy.70
  291.2 6.0 select_convert_fusion.3
  297.2 2.5 fusion.28
  302.0 7.9 %select_convert_fusion.2 = (bf16[4,512,1024]{2,1,0:T(8,128)(2,1)S(1)}, f32[4,512,1024]{2,1,0:T(8,128)}) fusion(pred[512,1024]{1,0:T(8,128)(4,1)} %get-tuple-element.24, bf16[4,4,1024,128]{3,2,0,1:T(8,128)(2,1)} %bitcast.79, bf16[4,1024,128]{2,1,0:T(8,128)(2,1)} %copy-done.12), kind=kOutput, calls=%fused_computation.11 | convolution fusion | flops 553648128 | bytes 14680064 | tf_op jit(solution)/shard_map/hqe,hke->hqk/dot_general | solution.py:89
  309.9 2.0 copy-done.8
  311.9 3.8 fusion.27
  315.7 2.6 copy.48
  318.3 2.0 multiply_reduce_fusion.3
  320.3 4.0 fusion.20
  324.4 3.3 slice_multiply_fusion
  330.0 6.9 %select_convert_fusion.1 = bf16[4,512,1024]{2,1,0:T(8,128)(2,1)S(1)} fusion(f32[4,512,1024]{2,1,0:T(8,128)} %get-tuple-element.41, pred[512,1024]{1,0:T(8,128)(4,1)S(1)} %copy-done.16, bf16[4,512,128]{2,1,0:T(8,128)(2,1)S(1)} %get-tuple-element.20, bf16[4,4,1024,128]{3,2,0,1:T(8,128)(2,1)S(1)} %bitcast.81), kind=kOutput, calls=%fused_computation.10 | convolution fusion | flops 562036736 | bytes 14680064 | tf_op jit(solution)/shard_map/hqe,hke->hqk/dot_general | solution.py:109
  342.0 6.7 %select_convert_fusion = bf16[4,512,1024]{2,1,0:T(8,128)(2,1)S(1)} fusion(f32[4,512,1024]{2,1,0:T(8,128)} %get-tuple-element.37, pred[512,1024]{1,0:T(8,128)(4,1)S(1)} %copy-done.14, bf16[4,512,128]{2,1,0:T(8,128)(2,1)S(1)} %get-tuple-element.19, bf16[4,4,1024,128]{3,2,0,1:T(8,128)(2,1)S(1)} %bitcast.83), kind=kOutput, calls=%fused_computation.9 | convolution fusion | flops 562036736 | bytes 14680064 | tf_op jit(solution)/shard_map/hqe,hke->hqk/dot_general | solution.py:109
  351.9 3.8 maximum_bitcast_fusion
  355.7 12.0 %copy.57 = f32[1024,4,4,128]{3,2,1,0:T(4,128)} copy(f32[1024,4,4,128]{3,0,1,2:T(8,128)} %maximum_bitcast_fusion) | data formatting | bytes 16777216 | tf_op jit(solution)/shard_map/transpose | solution.py:131
  367.7 10.3 %reshape.319 = f32[1024,2048]{1,0:T(8,128)} reshape(f32[1024,4,4,128]{3,2,1,0:T(4,128)} %copy.57) | data formatting | bytes 16777216 | tf_op jit(solution)/shard_map/reshape | solution.py:132
  378.0 7.5 %multiply_convert_fusion = bf16[1024,2048]{1,0:T(8,128)(2,1)S(1)} fusion(f32[1024,2048]{1,0:T(8,128)} %reshape.319, f32[1024,2048]{1,0:T(8,128)} %get-tuple-element.35), kind=kLoop, calls=%fused_computation.8 | loop fusion | flops 18874368 | bytes 20971520 | tf_op jit(solution)/shard_map/convert_element_type | solution.py:134
  387.4 6.1 fusion.31
  396.2 4.2 convolution_convert_fusion.1
  400.7 8.8 %convolution_convert_fusion = bf16[1024,2048]{1,0:T(8,128)(2,1)} fusion(bf16[1024,2048]{1,0:T(8,128)(2,1)} %copy-done.7, bf16[1024,1024]{1,0:T(8,128)(2,1)S(1)} %copy-done, f32[1024]{0:T(1024)S(1)} %add_rsqrt_fusion.2, f32[1024]{0:T(1024)S(1)} %broadcast_multiply_fusion.8), kind=kOutput, calls=%fused_computation.23 | convolution fusion | flops 4301258752 | bytes 10493952 | tf_op jit(solution)/shard_map/dot_general | solution.py:146
  409.6 2.5 fusion
  412.1 34.4 %reduce-scatter.4.cloned.1.call-done = f32[1024,512]{1,0:T(8,128)} async-done(((f32[1024,1024]{1,0:T(8,128)}), f32[1024,512]{1,0:T(8,128)}) %reduce-scatter.4.cloned.1.call-update) | async-done | bytes 2097168 | tf_op jit(solution)/shard_map/reduce_scatter | solution.py:158
  446.5 2.6 fusion.24
  449.1 5.0 all-reduce.1
  454.2 2.8 add_convert_fusion
  457.0 9.2 %gather_fusion = bf16[2048,512]{1,0:T(8,128)(2,1)} fusion(bf16[1024,512]{1,0:T(8,128)(2,1)S(1)} %add_convert_fusion, s32[2048]{0:T(1024)S(1)} %broadcast_clamp_fusion), kind=kCustom, calls=%fused_computation.2 | custom fusion | bytes 4202496 | tf_op jit(solution)/shard_map/jit(_take)/gather | solution.py:169
  469.7 5.1 scatter_fusion.2
  474.8 5.6 all-to-all-start.2
  480.5 49.0 %reduce-scatter.8.cloned.1.call-done = bf16[64,512]{1,0:T(8,128)(2,1)} async-done(((bf16[1024,512]{1,0:T(8,128)(2,1)}), bf16[64,512]{1,0:T(8,128)(2,1)}) %reduce-scatter.8.cloned.1.call-update) | async-done | bytes 65552 | tf_op jit(solution)/shard_map/reduce_scatter | solution.py:136
  530.9 72.8 %reduce-scatter.6.cloned.1.call-done = bf16[64,2048]{1,0:T(8,128)(2,1)} async-done(((bf16[1024,2048]{1,0:T(8,128)(2,1)}), bf16[64,2048]{1,0:T(8,128)(2,1)}) %reduce-scatter.6.cloned.1.call-update) | async-done | bytes 262160 | tf_op jit(solution)/shard_map/reduce_scatter | solution.py:145
  607.6 3.2 broadcast_select_fusion
  (128 shorter events, 41.2 us)
Async XLA Ops:
  23.8 7.4 %copy-start.23 = (s32[16]{0:T(128)}, s32[16]{0:T(128)S(1)}, u32[]{:S(2)}) copy-start(s32[16]{0:T(128)S(1)} %select_reduce_fusion.2) | copy-start | bytes 196
  23.8 12.7 %copy-start.17 = (s32[16]{0:T(128)}, s32[16]{0:T(128)S(1)}, u32[]{:S(2)}) copy-start(s32[16]{0:T(128)S(1)} %fusion.21) | copy-start | bytes 196
  31.2 44.8 %all-to-all-start = ((bf16[16,128,512]{2,1,0:T(8,128)(2,1)}), bf16[16,128,512]{2,1,0:T(8,128)(2,1)S(1)}, u32[]{:S(2)}, u32[]{:S(2)}) async-start(bf16[16,128,512]{2,1,0:T(8,128)(2,1)} %scatter_fusion), calls=%async_computation | async-start | bytes 4194304 | tf_op jit(solution)/shard_map/all_to_all | solution.py:45
  36.4 51.6 %copy-start.21 = (s32[16]{0:T(128)S(1)}, s32[16]{0:T(128)}, u32[]{:S(2)}) copy-start(s32[16]{0:T(128)} %param.13) | copy-start | bytes 196
  36.4 51.9 %copy-start.25 = (s32[16]{0:T(128)S(1)}, s32[16]{0:T(128)}, u32[]{:S(2)}) copy-start(s32[16]{0:T(128)} %param.12) | copy-start | bytes 196
  76.0 54.5 %all-to-all-start.1 = ((bf16[16,128,512]{2,1,0:T(8,128)(2,1)}), bf16[16,128,512]{2,1,0:T(8,128)(2,1)}, u32[]{:S(2)}, u32[]{:S(2)}) async-start(bf16[16,128,512]{2,1,0:T(8,128)(2,1)} %scatter_fusion.1), calls=%async_computation.1 | async-start | bytes 4194304 | tf_op jit(solution)/shard_map/all_to_all | solution.py:44
  87.2 58.4 %all-gather.7.cloned.1.call-start = ((), (), s32[]{:S(2)}) async-start(), calls=%async_computation.7 | async-start | bytes 1114112 | tf_op jit(solution)/shard_map/all_gather | solution.py:56
  88.0 92.8 %all-gather.5.cloned.1.call-start = ((), (), s32[]{:S(2)}) async-start(), calls=%async_computation.6 | async-start | bytes 3145728 | tf_op jit(solution)/shard_map/all_gather | solution.py:53
  88.3 0.5 copy-start.19
  138.0 77.5 %all-gather.9.cloned.1.call-start = ((), (), s32[]{:S(2)}) async-start(), calls=%async_computation.8 | async-start | bytes 3145728 | tf_op jit(solution)/shard_map/all_gather | solution.py:52
  138.7 129.5 %all-gather.11.cloned.1.call-start = ((), (), s32[]{:S(2)}) async-start(), calls=%async_computation.9 | async-start | bytes 4456448 | tf_op jit(solution)/shard_map/all_gather | solution.py:55
  139.3 307.2 %reduce-scatter.4.cloned.1.call-start = ((), (), s32[]{:S(2)}) async-start(), calls=%async_computation.10 | async-start | bytes 6291456 | tf_op jit(solution)/shard_map/reduce_scatter | solution.py:158
  141.3 149.8 %copy-start.15 = (pred[512,1024]{1,0:T(8,128)(4,1)}, pred[512,1024]{1,0:T(8,128)(4,1)S(1)}, u32[]{:S(2)}) copy-start(pred[512,1024]{1,0:T(8,128)(4,1)S(1)} %get-tuple-element.25) | copy-start | bytes 1572868
  215.5 52.8 %copy-start = (bf16[1024,1024]{1,0:T(8,128)(2,1)S(1)}, bf16[1024,1024]{1,0:T(8,128)(2,1)}, u32[]{:S(2)}) copy-start(bf16[1024,1024]{1,0:T(8,128)(2,1)} %all-gather.9.cloned.1.call-done) | copy-start | bytes 6291460
  289.8 7.4 %copy-start.3 = (bf16[1024,4,4,128]{3,0,1,2:T(8,128)(2,1)}, bf16[1024,4,4,128]{3,0,1,2:T(8,128)(2,1)S(1)}, u32[]{:S(2)}) copy-start(bf16[1024,4,4,128]{3,0,1,2:T(8,128)(2,1)S(1)} %copy.70) | copy-start | bytes 12582916
  291.2 6.1 copy-start.12
  297.2 2.5 copy-start.10
  309.9 2.0 copy-start.8
  318.3 6.1 copy-start.1
  318.3 6.2 copy-start.2
  318.3 6.2 copy-start.6
  324.4 3.3 copy-start.11
  327.7 2.2 copy-start.4
  327.7 2.3 copy-start.16
  336.9 1.3 copy-start.13
  338.2 2.2 copy-start.9
  340.4 1.6 copy-start.14
  378.0 9.5 %copy-start.27 = (bf16[1024,2048]{1,0:T(8,128)(2,1)S(1)}, bf16[1024,2048]{1,0:T(8,128)(2,1)}, u32[]{:S(2)}) copy-start(bf16[1024,2048]{1,0:T(8,128)(2,1)} %all-gather.11.cloned.1.call-done) | copy-start | bytes 12582916
  385.4 2.0 copy-start.7
  393.6 135.9 %reduce-scatter.8.cloned.1.call-start = ((), (), s32[]{:S(2)}) async-start(), calls=%async_computation.12 | async-start | bytes 1114112 | tf_op jit(solution)/shard_map/reduce_scatter | solution.py:136
  396.2 4.3 copy-start.26
  396.2 4.3 copy-start.20
  396.2 4.3 copy-start.22
  400.5 203.3 %reduce-scatter.6.cloned.1.call-start = ((), (), s32[]{:S(2)}) async-start(), calls=%async_computation.11 | async-start | bytes 4456448 | tf_op jit(solution)/shard_map/reduce_scatter | solution.py:145
  409.6 44.6 %copy-start.5 = (bf16[1024,512]{1,0:T(8,128)(2,1)S(1)}, bf16[1024,512]{1,0:T(8,128)(2,1)}, u32[]{:S(2)}) copy-start(bf16[1024,512]{1,0:T(8,128)(2,1)} %get-tuple-element.32) | copy-start | bytes 3145732
  469.7 10.8 %copy-start.18 = (s32[16]{0:T(128)S(1)}, s32[16]{0:T(128)}, u32[]{:S(2)}) copy-start(s32[16]{0:T(128)} %copy-done.17) | copy-start | bytes 196
  469.7 10.8 %copy-start.24 = (s32[16]{0:T(128)S(1)}, s32[16]{0:T(128)}, u32[]{:S(2)}) copy-start(s32[16]{0:T(128)} %copy-done.23) | copy-start | bytes 196
  474.8 130.7 %all-to-all-start.2 = ((bf16[16,128,512]{2,1,0:T(8,128)(2,1)}), bf16[16,128,512]{2,1,0:T(8,128)(2,1)S(1)}, u32[]{:S(2)}, u32[]{:S(2)}) async-start(bf16[16,128,512]{2,1,0:T(8,128)(2,1)} %scatter_fusion.2), calls=%async_computation.3 | async-start | bytes 4194304 | tf_op jit(solution)/shard_map/all_to_all | solution.py:172
Sparse Core Ops, SparseCore 0:
  90.2 55.3 all-gather.6
  147.2 33.5 all-gather.4
  182.3 33.1 all-gather.8
  217.5 50.7 all-gather.10
  393.7 52.7 reduce-scatter.3
  450.4 78.9 reduce-scatter.7
  533.3 70.4 reduce-scatter.5
where the time goes:
time: 622 us; the launch traced here: 618 us
  waiting for transfers between devices  347 us (56%)
  local copies, waits for them, and re-layouts  92.1 us (15%)
  matrix products  75.8 us (12%)
  other arithmetic  47.4 us (8%)
  starting transfers between devices  21.1 us (3%)
  blocking collectives  18.7 us (3%)
  between operations  15.6 us (3%)
    reduce_scatter x1, waiting for transfers between devices, local(): lax.psum_scatter(lax.dot_general(columns, dz, (((0,), (0,)), ((), ())), p...  72.8 us
    reduce_scatter x1, waiting for transfers between devices, local(): lax.psum_scatter(lax.dot_general(columns, hb, (((0,), (0,)), ((), ())), p...  49 us
    all_gather x1, waiting for transfers between devices, local(): w_in_cols = lax.all_gather(w_in, 'user', axis=0, tiled=True)  48.4 us
    all_to_all x1, waiting for transfers between devices, local(): lax.all_to_all(send_x, 'user', split_axis=0, concat_axis=0, tiled=True)  37.7 us
    all_gather x1, waiting for transfers between devices, local(): lax.all_gather(dp, 'tensor', axis=1, tiled=True)  35.2 us
    reduce_scatter x1, waiting for transfers between devices, local(): dn_share = lax.psum_scatter(dn, 'tensor', scatter_dimension=1, tiled=True)  34.4 us
    all_to_all x1, waiting for transfers between devices, local(): lax.all_to_all(send_d, 'user', split_axis=0, concat_axis=0, tiled=True)  33.6 us
    all_gather x1, waiting for transfers between devices, local(): lax.all_gather(xp, 'tensor', axis=1, tiled=True)  29.7 us
  transfers between devices with their start and end apart: 10, of which 9 were waited for; matrix products, arithmetic and copies ran while one was open for 12% of the time, Pallas kernels for 0%

commit v1 on v0

v1 whole, which is shorter than its diff:
```python
import functools

import jax
import jax.numpy as jnp
from jax import lax
from jax.experimental import pallas as pl
from jax.experimental.pallas import tpu as pltpu
from jax.sharding import PartitionSpec as P

HEAD_DIM = 128
SEQ_LEN = 128
GROUPS = 4
TILE = 2

eps = 1e-05
f32 = jnp.float32
bf16 = jnp.bfloat16


def dot_nn(a, b):
    return lax.dot_general(a, b, (((1,), (0,)), ((), ())), preferred_element_type=f32)


def dot_nt(a, b):
    return lax.dot_general(a, b, (((1,), (1,)), ((), ())), preferred_element_type=f32)


def dot_tn(a, b):
    return lax.dot_general(a, b, (((0,), (0,)), ((), ())), preferred_element_type=f32)


def sigmoid(t):
    return 0.5 * jnp.tanh(0.5 * t) + 0.5


def row_mean(t):
    return jnp.mean(t, axis=1, keepdims=True)


def history_pass(u, v, q, k, dh, causal):
    scale = HEAD_DIM ** (-0.5)
    s = dot_nt(q, k) * scale
    sig = sigmoid(s)
    silu = s * sig
    attn = jnp.where(causal, silu * (1.0 / SEQ_LEN), 0.0).astype(bf16)
    y = dot_nn(attn, v)
    cen = y - row_mean(y)
    rstd = lax.rsqrt(row_mean(cen * cen) + eps)
    yn = cen * rstd
    uf = u.astype(f32)
    hb = (yn * uf).astype(bf16)
    grad_u = dh * yn
    dyn = dh * uf
    dy = ((dyn - row_mean(dyn) - yn * row_mean(dyn * yn)) * rstd).astype(bf16)
    grad_a = dot_nt(dy, v)
    grad_v = dot_tn(attn, dy)
    slope = sig + silu * (1.0 - sig)
    grad_s = jnp.where(causal, grad_a * slope * (scale / SEQ_LEN), 0.0).astype(bf16)
    grad_q = dot_nn(grad_s, k)
    grad_k = dot_tn(grad_s, q)
    return hb, (grad_u, grad_v, grad_q, grad_k)


def group_kernel(first, last, heads, parts, *refs):
    refs = list(refs)
    lens_ref, part_ref, xo_ref, xr_ref, do_ref, dr_ref, w_hbm = refs[:7]
    refs = refs[7:]
    acc_hbm = None if first else refs.pop(0)
    gx_ref, bs_ref, grad_hbm, w_s, acc_s, nb_s, dm_s, dz_s, hb_s, out_s, sems = refs
    rows, own = xo_ref.shape
    width = own * parts
    cols_in = heads * 4 * HEAD_DIM
    cols = cols_in + heads * HEAD_DIM
    me = part_ref[0]

    def place(p):
        return pl.ds(pl.multiple_of(lax.rem(me + p, parts) * own, own), own)

    loads = []
    for p in range(parts):
        loads.append(
            pltpu.make_async_copy(
                w_hbm.at[place(p)], w_s.at[pl.ds(p * own, own)], sems.at[p]
            )
        )
        loads[-1].start()
    if not first:
        acc_load = pltpu.make_async_copy(acc_hbm, acc_s, sems.at[parts])
        acc_load.start()

    tr = min(TILE * SEQ_LEN, rows)
    causal = lax.broadcasted_iota(jnp.int32, (SEQ_LEN, SEQ_LEN), 0) >= lax.broadcasted_iota(
        jnp.int32, (SEQ_LEN, SEQ_LEN), 1
    )
    position = lax.broadcasted_iota(jnp.int32, (SEQ_LEN, 1), 0)

    for copy in loads:
        copy.wait()

    @pl.loop(0, rows // tr)
    def _(i):
        here = pl.ds(pl.multiple_of(i * tr, tr), tr)
        xo = xo_ref[here, :].astype(f32)
        xr = xr_ref[here, :].astype(f32)
        mean = (jnp.sum(xo, axis=1, keepdims=True) + jnp.sum(xr, axis=1, keepdims=True)) / width
        xo = xo - mean
        xr = xr - mean
        var = (
            jnp.sum(xo * xo, axis=1, keepdims=True) + jnp.sum(xr * xr, axis=1, keepdims=True)
        ) / width
        rstd = lax.rsqrt(var + eps)
        nb_s[here, :own] = (xo * rstd).astype(bf16)
        nb_s[here, own:] = (xr * rstd).astype(bf16)
        valid = jnp.concatenate(
            [position < lens_ref[i * (tr // SEQ_LEN) + n] for n in range(tr // SEQ_LEN)], axis=0
        )
        dm_s[here, :own] = jnp.where(valid, do_ref[here, :].astype(f32), 0.0).astype(bf16)
        dm_s[here, own:] = jnp.where(valid, dr_ref[here, :].astype(f32), 0.0).astype(bf16)
        dh = dot_nn(dm_s[here, :], w_s[:, cols_in:])
        for h in range(heads):
            c = h * 4 * HEAD_DIM
            z = dot_nn(nb_s[here, :], w_s[:, c : c + 4 * HEAD_DIM])
            sig = sigmoid(z)
            silu = z * sig
            slope = sig + silu * (1.0 - sig)
            g = silu.astype(bf16)
            for n in range(tr // SEQ_LEN):
                a, b = n * SEQ_LEN, (n + 1) * SEQ_LEN
                u, v, q, k = [g[a:b, e * HEAD_DIM : (e + 1) * HEAD_DIM] for e in range(4)]
                hb, grads = history_pass(
                    u, v, q, k, dh[a:b, h * HEAD_DIM : (h + 1) * HEAD_DIM], causal
                )
                there = pl.ds(pl.multiple_of(i * tr + a, SEQ_LEN), SEQ_LEN)
                hb_s[there, h * HEAD_DIM : (h + 1) * HEAD_DIM] = hb
                for e in range(4):
                    dz_s[there, c + e * HEAD_DIM : c + (e + 1) * HEAD_DIM] = (
                        grads[e] * slope[a:b, e * HEAD_DIM : (e + 1) * HEAD_DIM]
                    ).astype(bf16)
        dn = dot_nt(dz_s[here, :], w_s[:, :cols_in])
        no = xo * rstd
        nr = xr * rstd
        one = jnp.sum(dn, axis=1, keepdims=True) / width
        two = (
            jnp.sum(dn[:, :own] * no, axis=1, keepdims=True)
            + jnp.sum(dn[:, own:] * nr, axis=1, keepdims=True)
        ) / width
        gx_ref[here, :] = (
            dm_s[here, :own].astype(f32) + (dn[:, :own] - one - no * two) * rstd
        ).astype(bf16)
        bs_ref[here, :] = ((dn[:, own:] - one - nr * two) * rstd).astype(bf16)

    if not first:
        acc_load.wait()
    target = out_s if last else acc_s
    block = 4 * HEAD_DIM

    def add(lhs, rhs, lo, size):
        for r in range(0, width, 256):
            term = dot_tn(lhs[:, r : r + 256], rhs)
            if not first:
                term = term + acc_s[r : r + 256, pl.ds(lo, size)]
            target[r : r + 256, pl.ds(lo, size)] = term.astype(target.dtype)

    @pl.loop(0, cols_in // block)
    def _(j):
        lo = pl.multiple_of(j * block, block)
        add(nb_s, dz_s[:, pl.ds(lo, block)], lo, block)

    add(dm_s, hb_s[...], cols_in, cols - cols_in)

    stores = []
    if last:
        for p in range(parts):
            stores.append(
                pltpu.make_async_copy(
                    out_s.at[pl.ds(p * own, own)], grad_hbm.at[place(p)], sems.at[p]
                )
            )
    else:
        stores.append(pltpu.make_async_copy(acc_s, grad_hbm, sems.at[0]))
    for copy in stores:
        copy.start()
    for copy in stores:
        copy.wait()


def group_call(first, last, lens, part, xo, xr, do, dr, weights, acc):
    rows, own = xo.shape
    width, cols = weights.shape
    parts = width // own
    heads = cols // (5 * HEAD_DIM)
    whole = pl.BlockSpec(memory_space=pltpu.VMEM)
    smem = pl.BlockSpec(memory_space=pltpu.SMEM)
    anywhere = pl.BlockSpec(memory_space=pl.ANY)
    args = [lens, part, xo, xr, do, dr, weights] + ([] if first else [acc])
    specs = [smem, smem] + [whole] * 4 + [anywhere] * (1 if first else 2)
    kind = bf16 if last else f32
    flops = 2 * rows * width * cols * 2 + 2 * rows * width * heads * 4 * HEAD_DIM
    return pl.pallas_call(
        functools.partial(group_kernel, first, last, heads, parts),
        out_shape=(
            jax.ShapeDtypeStruct((rows, own), bf16),
            jax.ShapeDtypeStruct((rows, width - own), bf16),
            jax.ShapeDtypeStruct((width, cols), kind),
        ),
        in_specs=specs,
        out_specs=(whole, whole, anywhere),
        scratch_shapes=[
            pltpu.VMEM((width, cols), bf16),
            pltpu.VMEM((width, cols), f32),
            pltpu.VMEM((rows, width), bf16),
            pltpu.VMEM((rows, width), bf16),
            pltpu.VMEM((rows, heads * 4 * HEAD_DIM), bf16),
            pltpu.VMEM((rows, heads * HEAD_DIM), bf16),
            pltpu.VMEM((width, cols) if last else (16, 128), bf16),
            pltpu.SemaphoreType.DMA((parts + 1,)),
        ],
        compiler_params=pltpu.CompilerParams(vmem_limit_bytes=52 * 2**20),
        cost_estimate=pl.CostEstimate(
            flops=flops, bytes_accessed=16 * 2**20, transcendentals=rows * cols
        ),
    )(*args)


def exchange(block, tensor):
    if tensor == 2:
        return lax.ppermute(block, "tensor", [(0, 1), (1, 0)])
    own = block.shape[1]
    every = lax.all_gather(block, "tensor", axis=1, tiled=True)
    return jnp.roll(every, -lax.axis_index("tensor") * own, axis=1)[:, own:]


def give_back(block, own, tensor):
    if tensor == 2:
        return lax.ppermute(block, "tensor", [(0, 1), (1, 0)])
    every = jnp.concatenate([jnp.zeros((block.shape[0], own), block.dtype), block], axis=1)
    every = jnp.roll(every, lax.axis_index("tensor") * own, axis=1)
    return lax.psum_scatter(every, "tensor", scatter_dimension=1, tiled=True)


def local(events, cotangent, w_in, w_out, slot_source, slot_length):
    tensor = lax.axis_size("tensor")
    users = lax.axis_size("user")
    hist, seq_len, own = events.shape
    x = events.reshape(hist * seq_len, own)
    d = cotangent.reshape(hist * seq_len, own)
    rows = hist // GROUPS * seq_len
    xs = [x[g * rows : (g + 1) * rows] for g in range(GROUPS)]
    ds = [d[g * rows : (g + 1) * rows] for g in range(GROUPS)]
    pairs = []
    for g in range(GROUPS):
        pairs.append((exchange(xs[g], tensor), exchange(ds[g], tensor)))

    weights = lax.all_gather(
        jnp.concatenate([w_in, w_out], axis=1), "user", axis=0, tiled=True
    )
    table = lax.all_gather(slot_source * 256 + slot_length, "user", axis=0, tiled=True)
    table = table.reshape(users, hist)
    mine = (table // 256) == lax.axis_index("user")
    lens = jnp.sum(jnp.where(mine, table % 256, 0), axis=0)
    part = lax.axis_index("tensor").astype(jnp.int32).reshape(1)

    acc = None
    kept, sent = [], []
    for g in range(GROUPS):
        xr, dr = pairs[g]
        gx, bs, acc = group_call(
            g == 0,
            g == GROUPS - 1,
            lens[g * hist // GROUPS : (g + 1) * hist // GROUPS],
            part,
            xs[g],
            xr,
            ds[g],
            dr,
            weights,
            acc,
        )
        kept.append(gx)
        sent.append(give_back(bs, own, tensor))
    grads = lax.psum_scatter(acc, "user", scatter_dimension=0, tiled=True).astype(f32)
    grad_x = jnp.concatenate(
        [(k.astype(f32) + s.astype(f32)).astype(bf16) for k, s in zip(kept, sent)], axis=0
    )
    cols_in = w_in.shape[1]
    return (grad_x.reshape(hist, seq_len, own), grads[:, :cols_in], grads[:, cols_in:])


def solution(mesh):
    in_specs = (
        P("user", None, "tensor"),
        P("user", None, "tensor"),
        P("user", "tensor"),
        P("user", "tensor"),
        P("user"),
        P("user"),
    )
    out_specs = (P("user", None, "tensor"), P("user", "tensor"), P("user", "tensor"))
    return jax.shard_map(local, mesh=mesh, in_specs=in_specs, out_specs=out_specs, check_vma=False)
```

time: 622 us -> 277 us (0.45)
  waiting for transfers between devices: 347 us -> 102 us
  Pallas kernels: 0 us -> 117 us
  local copies, waits for them, and re-layouts: 92.1 us -> 10.5 us
  matrix products: 75.8 us -> 0 us
  other arithmetic: 47.4 us -> 3.87 us
    reduce_scatter x3 -> x1, waiting for transfers between devices: 156 us -> 26.1 us  [local(): lax.psum_scatter(acc, 'user', scatter_dimension=0, tiled=True).astype(f32)]
    pallas_call x0 -> x4, Pallas kernels: none -> 117 us  [group_call(): pl.pallas_call(functools.partial(group_kernel, first, last, heads, parts)...]
    all_gather x4 -> x1, waiting for transfers between devices: 118 us -> 29 us  [local(): lax.all_gather(jnp.concatenate([w_in, w_out], axis=1), 'user', axis=0, ti...]
    dot_general x17 -> x0, matrix products: 75.8 us -> none  [the longest x2 13.9 us: local(): jnp.einsum('hqe,hke->hqk', q_rows, kpart, preferred_element_type=jnp.floa...]
    all_to_all x3 -> x0, waiting for transfers between devices: 71.3 us -> none  [the longest x1 37.7 us: local(): lax.all_to_all(send_x, 'user', split_axis=0, concat_axis=0, tiled=True)]
    ppermute x0 -> x12, waiting for transfers between devices: none -> 47.1 us  [the longest x4 43 us: give_back(): return lax.ppermute(block, 'tensor', [(0, 1), (1, 0)])]
    reshape x4 -> x1, local copies, waits for them, and re-layouts: 23.1 us -> 0.08 us  [local(): table = table.reshape(users, hist)]
    gather x4 -> x0, local copies, waits for them, and re-layouts: 21 us -> none  [the longest x1 9.21 us: local(): jnp.take(dxp, rows_at.reshape(-1), axis=0)]
  transfers between devices with their start and end apart: 10 -> 14, of which waited for: 9 -> 7; matrix products, arithmetic and copies ran while one was open for 12% -> 2% of each run, Pallas kernels for 0% -> 32%
where the time goes in v1:
time: 277 us
  Pallas kernels  117 us (42%)
  waiting for transfers between devices  102 us (37%)
  starting transfers between devices  15.4 us (6%)
  between operations  14.9 us (5%)
  blocking collectives  12.7 us (5%)
  local copies, waits for them, and re-layouts  10.5 us (4%)
  other arithmetic  3.87 us (1%)
    pallas_call x4, Pallas kernels, group_call(): pl.pallas_call(functools.partial(group_kernel, first, last, heads, parts)...  117 us
    ppermute x4, waiting for transfers between devices, give_back(): return lax.ppermute(block, 'tensor', [(0, 1), (1, 0)])  43 us
    all_gather x1, waiting for transfers between devices, local(): lax.all_gather(jnp.concatenate([w_in, w_out], axis=1), 'user', axis=0, ti...  29 us
    reduce_scatter x1, waiting for transfers between devices, local(): lax.psum_scatter(acc, 'user', scatter_dimension=0, tiled=True).astype(f32)  26.1 us
    unnamed x1, blocking collectives  12.7 us
    ppermute x8, starting transfers between devices, exchange(): return lax.ppermute(block, 'tensor', [(0, 1), (1, 0)])  11.3 us
  transfers between devices with their start and end apart: 14, of which 7 were waited for; matrix products, arithmetic and copies ran while one was open for 2% of the time, Pallas kernels for 32%

profile of v1, /device:TPU:0, one launch (start us, length us, event | category | flops | bytes accessed | tf_op | source)
XLA Modules:
  0.0 276.8 jit_solution(16998084854289796126)
XLA Ops:
  7.2 0.0 all-gather.2.cloned.1.call-start
  7.2 1.8 pad_maximum_fusion.1
  9.0 0.0 all-gather.2.cloned.1.call-update
  9.0 0.0 copy-start.9
  9.0 0.0 reduce-scatter.2.cloned.1.call-start
  9.1 1.9 fusion.6
  11.0 3.0 %collective-permute-start = (bf16[512,512]{1,0:T(8,128)(2,1)S(1)}, bf16[512,512]{1,0:T(8,128)(2,1)}, u32[]{:S(2)}, u32[]{:S(2)}) collective-permute-start(bf16[512,512]{1,0:T(8,128)(2,1)S(1)} %bitcast.17), channel_id=1, source_target_pairs={{0,1},{1,0},{2,3},{3,2},{4,5},{5,4},{6,7},{7,6},{8,9},{9,8},{10,11... | collective-permute-start | bytes 1572872 | tf_op jit(solution)/shard_map/ppermute | solution.py:227
  14.0 1.2 fusion.5
  15.2 0.3 collective-permute-start.1
  15.4 1.8 collective-permute-start.3
  17.2 0.3 collective-permute-start.4
  17.5 1.8 collective-permute-start.6
  19.2 0.6 dynamic-slice
  20.5 0.1 add_dynamic-update-slice_fusion
  20.6 12.7 %all-reduce = s32[256]{0:T(256)S(1)} all-reduce(s32[256]{0:T(256)S(1)} %add_dynamic-update-slice_fusion), channel_id=1, replica_groups=mesh['user'=16,'tensor'=2] {'user'}, use_global_device_ids=true, to_apply=%add | all-reduce | flops 256 | bytes 2048
  33.3 0.1 reshape.25
  33.4 0.1 fusion.7
  33.5 0.6 collective-permute-start.7
  34.1 4.0 %collective-permute-done.1.refs_5_ = bf16[512,512]{1,0:T(8,128)(2,1)} collective-permute-done((bf16[512,512]{1,0:T(8,128)(2,1)S(1)}, bf16[512,512]{1,0:T(8,128)(2,1)}, u32[]{:S(2)}, u32[]{:S(2)}) %collective-permute-start.1) | collective-permute-done | bytes 524320 | tf_op jit(solution)/shard_map/ppermute | solution.py:227
  38.1 2.1 collective-permute-start.10
  40.1 29.0 %all-gather.2.cloned.1.call-done.refs_6_ = bf16[1024,2560]{1,0:T(8,128)(2,1)} async-done(((bf16[64,2560]{1,0:T(8,128)(2,1)}), bf16[1024,2560]{1,0:T(8,128)(2,1)}) %all-gather.2.cloned.1.call-update) | async-done | bytes 5242896 | tf_op jit(solution)/shard_map/all_gather | solution.py:254
  69.2 29.6 %shard_map.85 = (bf16[512,512]{1,0:T(8,128)(2,1)S(1)}, bf16[512,512]{1,0:T(8,128)(2,1)S(1)}, f32[1024,2560]{1,0:T(8,128)}) custom-call(s32[4]{0:T(128)S(1)} %get-tuple-element.35.refs_0_, s32[1]{0:T(128)} %bitcast.1.refs_1_, bf16[512,512]{1,0:T(8,128)(2,1)S(1)} %bitcast.18, bf16[512,512]{1,0:T(8,128)(2,1)} %collective-permute-done.refs_3_, ...), custom_call_target="tpu_custom_call" | custom-call | flops 7516192768 | bytes 16777216 | tf_op jit(solution)/shard_map/pallas_call | solution.py:199
  98.7 1.5 collective-permute-start.9
  100.3 29.9 %shard_map.86 = (bf16[512,512]{1,0:T(8,128)(2,1)S(1)}, bf16[512,512]{1,0:T(8,128)(2,1)S(1)}, f32[1024,2560]{1,0:T(8,128)}) custom-call(s32[4]{0:T(128)S(1)} %get-tuple-element.38.refs_0_, s32[1]{0:T(128)} %bitcast.1.refs_1_, bf16[512,512]{1,0:T(8,128)(2,1)S(1)} %bitcast.16, bf16[512,512]{1,0:T(8,128)(2,1)} %collective-permute-done.3.refs_3_, ...), custom_call_target="tpu_custom_call" | custom-call | flops 7516192768 | bytes 16777216 | tf_op jit(solution)/shard_map/pallas_call | solution.py:199
  130.2 29.7 %shard_map.87 = (bf16[512,512]{1,0:T(8,128)(2,1)S(1)}, bf16[512,512]{1,0:T(8,128)(2,1)S(1)}, f32[1024,2560]{1,0:T(8,128)}) custom-call(s32[4]{0:T(128)S(1)} %get-tuple-element.37.refs_0_, s32[1]{0:T(128)} %bitcast.1.refs_1_, bf16[512,512]{1,0:T(8,128)(2,1)S(1)} %bitcast.14, bf16[512,512]{1,0:T(8,128)(2,1)} %collective-permute-done.6.refs_3_, ...), custom_call_target="tpu_custom_call" | custom-call | flops 7516192768 | bytes 16777216 | tf_op jit(solution)/shard_map/pallas_call | solution.py:199
  160.0 0.8 copy-done.2
  160.8 0.8 copy-done.8
  161.6 28.0 %shard_map.88 = (bf16[512,512]{1,0:T(8,128)(2,1)S(1)}, bf16[512,512]{1,0:T(8,128)(2,1)S(1)}, bf16[1024,2560]{1,0:T(8,128)(2,1)}) custom-call(s32[4]{0:T(128)S(1)} %get-tuple-element.36.refs_0_, s32[1]{0:T(128)} %bitcast.1.refs_1_, bf16[512,512]{1,0:T(8,128)(2,1)S(1)} %bitcast.12, bf16[512,512]{1,0:T(8,128)(2,1)} %copy-done.8, ...), custom_call_target="tpu_custom_call" | custom-call | flops 7516192768 | bytes 16777216 | tf_op jit(solution)/shard_map/pallas_call | solution.py:199
  189.6 0.0 copy-start.3
  189.6 0.8 copy-done.3
  190.4 0.0 reduce-scatter.2.cloned.1.call-update
  190.4 1.0 copy-done.1
  191.4 0.5 collective-permute-start.5
  191.9 1.5 collective-permute-start.8
  193.5 0.5 collective-permute-start.11
  193.9 1.5 collective-permute-start.2
  195.5 10.7 %collective-permute-done.5 = bf16[512,512]{1,0:T(8,128)(2,1)S(1)} collective-permute-done((bf16[512,512]{1,0:T(8,128)(2,1)S(1)}, bf16[512,512]{1,0:T(8,128)(2,1)S(1)}, u32[]{:S(2)}, u32[]{:S(2)}) %collective-permute-start.5) | collective-permute-done | bytes 524320 | tf_op jit(solution)/shard_map/ppermute | solution.py:235
  206.2 0.1 add_convert_fusion.2
  206.4 11.1 %collective-permute-done.8 = bf16[512,512]{1,0:T(8,128)(2,1)S(1)} collective-permute-done((bf16[512,512]{1,0:T(8,128)(2,1)}, bf16[512,512]{1,0:T(8,128)(2,1)S(1)}, u32[]{:S(2)}, u32[]{:S(2)}) %collective-permute-start.8) | collective-permute-done | bytes 524320 | tf_op jit(solution)/shard_map/ppermute | solution.py:235
  217.5 0.1 add_convert_fusion.1
  217.6 11.1 %collective-permute-done.11 = bf16[512,512]{1,0:T(8,128)(2,1)S(1)} collective-permute-done((bf16[512,512]{1,0:T(8,128)(2,1)}, bf16[512,512]{1,0:T(8,128)(2,1)S(1)}, u32[]{:S(2)}, u32[]{:S(2)}) %collective-permute-start.11) | collective-permute-done | bytes 524320 | tf_op jit(solution)/shard_map/ppermute | solution.py:235
  228.7 0.1 add_convert_fusion
  228.8 10.1 %collective-permute-done.2 = bf16[512,512]{1,0:T(8,128)(2,1)S(1)} collective-permute-done((bf16[512,512]{1,0:T(8,128)(2,1)S(1)}, bf16[512,512]{1,0:T(8,128)(2,1)S(1)}, u32[]{:S(2)}, u32[]{:S(2)}) %collective-permute-start.2) | collective-permute-done | bytes 524320 | tf_op jit(solution)/shard_map/ppermute | solution.py:235
  238.9 0.1 add_convert_fusion.3
  239.1 1.5 pad_maximum_fusion
  240.5 26.1 %reduce-scatter.2.cloned.1.call-done = bf16[64,2560]{1,0:T(8,128)(2,1)} async-done(((bf16[1024,2560]{1,0:T(8,128)(2,1)}), bf16[64,2560]{1,0:T(8,128)(2,1)}) %reduce-scatter.2.cloned.1.call-update) | async-done | bytes 327696 | tf_op jit(solution)/shard_map/reduce_scatter | solution.py:281
  266.7 1.8 slice.88
  268.4 1.5 slice.89
  (23 shorter events, 0.1 us)
Async XLA Ops:
  7.2 62.0 %all-gather.2.cloned.1.call-start = ((), (), s32[]{:S(2)}) async-start(), calls=%async_computation.1 | async-start | bytes 5570560 | tf_op jit(solution)/shard_map/all_gather | solution.py:254
  9.0 10.2 %copy-start.9 = (u32[32]{0:T(128)S(1)}, u32[32]{0:T(128)}, u32[]{:S(2)}) copy-start(u32[32]{0:T(128)} %constant.40) | copy-start | bytes 388
  9.0 11.5 %copy-start.6 = (s32[16]{0:T(128)S(1)}, s32[16]{0:T(128)}, u32[]{:S(2)}) copy-start(s32[16]{0:T(128)} %param.11) | copy-start | bytes 196
  9.0 11.5 %copy-start.7 = (s32[16]{0:T(128)S(1)}, s32[16]{0:T(128)}, u32[]{:S(2)}) copy-start(s32[16]{0:T(128)} %param.10) | copy-start | bytes 196
  9.0 257.6 %reduce-scatter.2.cloned.1.call-start = ((), (), s32[]{:S(2)}) async-start(), calls=%async_computation.2 | async-start | bytes 5570560 | tf_op jit(solution)/shard_map/reduce_scatter | solution.py:281
  9.1 4.9 %copy-start.4 = (bf16[16,128,512]{2,1,0:T(8,128)(2,1)S(1)}, bf16[16,128,512]{2,1,0:T(8,128)(2,1)}, u32[]{:S(2)}) copy-start(bf16[16,128,512]{2,1,0:T(8,128)(2,1)} %param.7) | copy-start | bytes 6291460
  11.0 22.5 %collective-permute-start = (bf16[512,512]{1,0:T(8,128)(2,1)S(1)}, bf16[512,512]{1,0:T(8,128)(2,1)}, u32[]{:S(2)}, u32[]{:S(2)}) collective-permute-start(bf16[512,512]{1,0:T(8,128)(2,1)S(1)} %bitcast.17), channel_id=1, source_target_pairs={{0,1},{1,0},{2,3},{3,2},{4,5},{5,4},{6,7},{7,6},{8,9},{9,8},{10,11... | collective-permute-start | bytes 1572872 | tf_op jit(solution)/shard_map/ppermute | solution.py:227
  15.2 54.0 %copy-start.5 = (bf16[4,128,512]{2,1,0:T(8,128)(2,1)}, bf16[4,128,512]{2,1,0:T(8,128)(2,1)S(1)}, u32[]{:S(2)}) copy-start(bf16[4,128,512]{2,1,0:T(8,128)(2,1)S(1)} %get-tuple-element.27) | copy-start | bytes 1572868
  15.2 22.9 %collective-permute-start.1 = (bf16[512,512]{1,0:T(8,128)(2,1)S(1)}, bf16[512,512]{1,0:T(8,128)(2,1)}, u32[]{:S(2)}, u32[]{:S(2)}) collective-permute-start(bf16[512,512]{1,0:T(8,128)(2,1)S(1)} %bitcast.20), channel_id=1, source_target_pairs={{0,1},{1,0},{2,3},{3,2},{4,5},{5,4},{6,7},{7,6},{8,9},{9,8},{10,11... | collective-permute-start | bytes 1572872 | tf_op jit(solution)/shard_map/ppermute | solution.py:227
  15.4 83.3 %collective-permute-start.3 = (bf16[512,512]{1,0:T(8,128)(2,1)S(1)}, bf16[512,512]{1,0:T(8,128)(2,1)}, u32[]{:S(2)}, u32[]{:S(2)}) collective-permute-start(bf16[512,512]{1,0:T(8,128)(2,1)S(1)} %bitcast.15), channel_id=1, source_target_pairs={{0,1},{1,0},{2,3},{3,2},{4,5},{5,4},{6,7},{7,6},{8,9},{9,8},{10,11... | collective-permute-start | bytes 1572872 | tf_op jit(solution)/shard_map/ppermute | solution.py:227
  17.2 83.1 %collective-permute-start.4 = (bf16[512,512]{1,0:T(8,128)(2,1)}, bf16[512,512]{1,0:T(8,128)(2,1)}, u32[]{:S(2)}, u32[]{:S(2)}) collective-permute-start(bf16[512,512]{1,0:T(8,128)(2,1)} %bitcast.5.refs_4_), channel_id=1, source_target_pairs={{0,1},{1,0},{2,3},{3,2},{4,5},{5,4},{6,7},{7,6},{8,9},{9,8},{10,11... | collective-permute-start | bytes 1572872 | tf_op jit(solution)/shard_map/ppermute | solution.py:227
  17.5 112.7 %collective-permute-start.6 = (bf16[512,512]{1,0:T(8,128)(2,1)S(1)}, bf16[512,512]{1,0:T(8,128)(2,1)}, u32[]{:S(2)}, u32[]{:S(2)}) collective-permute-start(bf16[512,512]{1,0:T(8,128)(2,1)S(1)} %bitcast.13), channel_id=1, source_target_pairs={{0,1},{1,0},{2,3},{3,2},{4,5},{5,4},{6,7},{7,6},{8,9},{9,8},{10,11... | collective-permute-start | bytes 1572872 | tf_op jit(solution)/shard_map/ppermute | solution.py:227
  33.5 96.7 %collective-permute-start.7 = (bf16[512,512]{1,0:T(8,128)(2,1)}, bf16[512,512]{1,0:T(8,128)(2,1)}, u32[]{:S(2)}, u32[]{:S(2)}) collective-permute-start(bf16[512,512]{1,0:T(8,128)(2,1)} %bitcast.7.refs_4_), channel_id=1, source_target_pairs={{0,1},{1,0},{2,3},{3,2},{4,5},{5,4},{6,7},{7,6},{8,9},{9,8},{10,11... | collective-permute-start | bytes 1572872 | tf_op jit(solution)/shard_map/ppermute | solution.py:227
  38.1 122.7 %collective-permute-start.10 = (bf16[512,512]{1,0:T(8,128)(2,1)}, bf16[512,512]{1,0:T(8,128)(2,1)}, u32[]{:S(2)}, u32[]{:S(2)}) collective-permute-start(bf16[512,512]{1,0:T(8,128)(2,1)} %bitcast.9.refs_4_), channel_id=1, source_target_pairs={{0,1},{1,0},{2,3},{3,2},{4,5},{5,4},{6,7},{7,6},{8,9},{9,8},{10,11... | collective-permute-start | bytes 1572872 | tf_op jit(solution)/shard_map/ppermute | solution.py:227
  98.7 62.0 %collective-permute-start.9 = (bf16[512,512]{1,0:T(8,128)(2,1)S(1)}, bf16[512,512]{1,0:T(8,128)(2,1)S(1)}, u32[]{:S(2)}, u32[]{:S(2)}) collective-permute-start(bf16[512,512]{1,0:T(8,128)(2,1)S(1)} %bitcast.11), channel_id=1, source_target_pairs={{0,1},{1,0},{2,3},{3,2},{4,5},{5,4},{6,7},{7,6},{8,9},{9,8},{10,11... | collective-permute-start | bytes 1572872 | tf_op jit(solution)/shard_map/ppermute | solution.py:227
  130.2 29.8 %copy-start = (bf16[512,512]{1,0:T(8,128)(2,1)}, bf16[512,512]{1,0:T(8,128)(2,1)S(1)}, u32[]{:S(2)}) copy-start(bf16[512,512]{1,0:T(8,128)(2,1)S(1)} %get-tuple-element.19) | copy-start | bytes 1572868
  160.0 0.8 copy-start.2
  160.8 0.8 copy-start.8
  189.6 0.8 copy-start.3
  190.4 1.0 copy-start.1
  191.4 14.8 %collective-permute-start.5 = (bf16[512,512]{1,0:T(8,128)(2,1)S(1)}, bf16[512,512]{1,0:T(8,128)(2,1)S(1)}, u32[]{:S(2)}, u32[]{:S(2)}) collective-permute-start(bf16[512,512]{1,0:T(8,128)(2,1)S(1)} %copy-done.1), channel_id=1, source_target_pairs={{0,1},{1,0},{2,3},{3,2},{4,5},{5,4},{6,7},{7,6},{8,9},{9,8},{10,11... | collective-permute-start | bytes 1572872 | tf_op jit(solution)/shard_map/ppermute | solution.py:235
  191.9 25.5 %collective-permute-start.8 = (bf16[512,512]{1,0:T(8,128)(2,1)}, bf16[512,512]{1,0:T(8,128)(2,1)S(1)}, u32[]{:S(2)}, u32[]{:S(2)}) collective-permute-start(bf16[512,512]{1,0:T(8,128)(2,1)} %copy-done.2), channel_id=1, source_target_pairs={{0,1},{1,0},{2,3},{3,2},{4,5},{5,4},{6,7},{7,6},{8,9},{9,8},{10,11... | collective-permute-start | bytes 1572872 | tf_op jit(solution)/shard_map/ppermute | solution.py:235
  193.5 35.2 %collective-permute-start.11 = (bf16[512,512]{1,0:T(8,128)(2,1)}, bf16[512,512]{1,0:T(8,128)(2,1)S(1)}, u32[]{:S(2)}, u32[]{:S(2)}) collective-permute-start(bf16[512,512]{1,0:T(8,128)(2,1)} %copy-done.3), channel_id=1, source_target_pairs={{0,1},{1,0},{2,3},{3,2},{4,5},{5,4},{6,7},{7,6},{8,9},{9,8},{10,11... | collective-permute-start | bytes 1572872 | tf_op jit(solution)/shard_map/ppermute | solution.py:235
  193.9 45.0 %collective-permute-start.2 = (bf16[512,512]{1,0:T(8,128)(2,1)S(1)}, bf16[512,512]{1,0:T(8,128)(2,1)S(1)}, u32[]{:S(2)}, u32[]{:S(2)}) collective-permute-start(bf16[512,512]{1,0:T(8,128)(2,1)S(1)} %get-tuple-element.16), channel_id=1, source_target_pairs={{0,1},{1,0},{2,3},{3,2},{4,5},{5,4},{6,7},{7,6},{8,9},{9,8},{10,11... | collective-permute-start | bytes 1572872 | tf_op jit(solution)/shard_map/ppermute | solution.py:235
Sparse Core Ops, SparseCore 0:
  10.3 58.8 all-gather.1
  190.5 76.0 reduce-scatter.1
